TPU v7x, 256 devices: a whole 4x4x8 slice. The times are simulated.
256 devices in a mesh: ctx: 8 (over x, core), tp: 32 (over z, y).
Axes of the slice: x: 4, y: 4, z: 8, core: 2. Of those that a mesh axis runs over, the one named last changes fastest.
Arguments:
- tokens: bfloat16 [2048, 8192], P('ctx', 'tp'), may hold values from -6 to 6
- in_weight: bfloat16 [3, 8192, 8192], P(None, 'ctx', 'tp'), may hold values from -0.0625 to 0.0625
- filter_spectrum: float32 [2, 16, 256, 8192], P(None, 'ctx', None, 'tp'), may hold values from -6 to 6
- skip_gain: float32 [8192], P('tp'), may hold values from -4 to 4
- out_weight: bfloat16 [8192, 8192], P(None, 'tp'), may hold values from -0.0625 to 0.0625
Outputs:
- mixed: bfloat16 [2048, 8192], P('ctx', 'tp')
All inputs are finite; a program needn't handle non-finite values.
Results may differ from a plain program's by a relative error of at most 0.007.
Values may be sent and summed in bfloat16 or wider, within the bound.
No kernel may reach another device: no remote copies, remote signals or barrier semaphores. Data moves between devices by JAX's collectives and lax.ppermute only.
A program may use at most 128 MiB of HBM per device.

v0:
```python
import math

import jax
import jax.numpy as jnp
from jax import lax
from jax.sharding import PartitionSpec as P


def mult_high(form, left, right):
    return jnp.einsum(
        form, left, right, precision=lax.Precision.HIGHEST, preferred_element_type=jnp.float32
    )


def spread_step(values):
    return lax.all_to_all(values, "ctx", split_axis=2, concat_axis=1, tiled=True)


def collect_step(values):
    return lax.all_to_all(values, "ctx", split_axis=1, concat_axis=2, tiled=True)


def shards(tokens, in_weight, filter_spectrum, skip_gain, out_weight):
    length, channels = tokens.shape
    groups = lax.axis_size("ctx")
    my_index = lax.axis_index("ctx")
    classes = 2 * groups
    stride = length // groups
    period = 2 * length * groups
    gathered = lax.all_gather(tokens, "tp", axis=1, tiled=True)
    summed = jnp.einsum(
        "td,idc->tic",
        gathered,
        lax.all_gather(in_weight, "ctx", axis=1, tiled=True),
        preferred_element_type=jnp.float32,
    )
    projected = summed.astype(jnp.bfloat16)
    outer_gate = projected[:, 0, :].astype(jnp.float32)
    inner_gate = projected[:, 1, :].astype(jnp.float32)
    value_part = projected[:, 2, :].astype(jnp.float32)
    driven = inner_gate * value_part
    class_index = jnp.arange(classes, dtype=jnp.int32)
    row_index = jnp.arange(length, dtype=jnp.int32)
    block_index = jnp.arange(groups, dtype=jnp.int32)
    small_angle = (
        2.0
        * math.pi
        / classes
        * (class_index[:, None] * block_index[None, :] % classes).astype(jnp.float32)
    )
    small_cos = jnp.cos(small_angle)
    small_sin = jnp.sin(small_angle)
    blocks_in = spread_step(driven.reshape(1, 1, length, channels))[0]
    first_real = mult_high("jq,qrc->jrc", small_cos, blocks_in)
    first_imag = -mult_high("jq,qrc->jrc", small_sin, blocks_in)
    local_rows = my_index * stride + jnp.arange(stride, dtype=jnp.int32)
    twist_angle = (
        2.0
        * math.pi
        / period
        * (class_index[:, None] * local_rows[None, :] % period).astype(jnp.float32)
    )
    twist_cos = jnp.cos(twist_angle)[:, :, None]
    twist_sin = jnp.sin(twist_angle)[:, :, None]
    turned_real = first_real * twist_cos + first_imag * twist_sin
    turned_imag = first_imag * twist_cos - first_real * twist_sin
    columns_in = collect_step(jnp.stack([turned_real, turned_imag]))
    big_angle = (
        2.0
        * math.pi
        / length
        * (row_index[:, None] * row_index[None, :] % length).astype(jnp.float32)
    )
    big_cos = jnp.cos(big_angle)
    big_sin = jnp.sin(big_angle)
    freq_real = mult_high("gr,jrc->jgc", big_cos, columns_in[0]) + mult_high(
        "gr,jrc->jgc", big_sin, columns_in[1]
    )
    freq_imag = mult_high("gr,jrc->jgc", big_cos, columns_in[1]) - mult_high(
        "gr,jrc->jgc", big_sin, columns_in[0]
    )
    filter_real = filter_spectrum[0]
    filter_imag = filter_spectrum[1]
    prod_real = freq_real * filter_real - freq_imag * filter_imag
    prod_imag = freq_real * filter_imag + freq_imag * filter_real
    back_real = mult_high("rg,jgc->jrc", big_cos, prod_real) - mult_high(
        "rg,jgc->jrc", big_sin, prod_imag
    )
    back_imag = mult_high("rg,jgc->jrc", big_sin, prod_real) + mult_high(
        "rg,jgc->jrc", big_cos, prod_imag
    )
    own_classes = 2 * my_index + jnp.arange(2, dtype=jnp.int32)
    untwist_angle = (
        2.0
        * math.pi
        / period
        * (own_classes[:, None] * row_index[None, :] % period).astype(jnp.float32)
    )
    untwist_cos = jnp.cos(untwist_angle)[:, :, None]
    untwist_sin = jnp.sin(untwist_angle)[:, :, None]
    reverted_real = back_real * untwist_cos - back_imag * untwist_sin
    reverted_imag = back_real * untwist_sin + back_imag * untwist_cos
    returned = spread_step(jnp.stack([reverted_real, reverted_imag]))
    inverse_blocks = (
        mult_high("jq,jrc->qrc", small_cos, returned[0])
        - mult_high("jq,jrc->qrc", small_sin, returned[1])
    ) * (1.0 / period)
    convolved = collect_step(inverse_blocks[None]).reshape(length, channels)
    gated = (outer_gate * (convolved + skip_gain * driven)).astype(jnp.bfloat16)
    mixed = jnp.dot(
        lax.all_gather(gated, "tp", axis=1, tiled=True),
        out_weight,
        preferred_element_type=jnp.float32,
    )
    return mixed.astype(jnp.bfloat16)


def solution(mesh):
    placed = (
        P("ctx", "tp"),
        P(None, "ctx", "tp"),
        P(None, "ctx", None, "tp"),
        P("tp"),
        P(None, "tp"),
    )
    return jax.shard_map(
        shards, mesh=mesh, in_specs=placed, out_specs=P("ctx", "tp"), check_vma=False
    )
```

profile of v0, /device:TPU:24, one launch (start us, length us, event | category | flops | bytes accessed | tf_op | source)
XLA Modules:
  0.0 354.0 jit_solution(18442023640341271532)
XLA Ops:
  6.5 0.7 all-gather.4.cloned.1.call-update
  7.3 0.0 all-gather.6.cloned.1.call-start
  7.3 0.7 all-gather.6.cloned.1.call-update
  8.0 88.4 %all-gather.4.cloned.1.call-done = bf16[256,8192]{1,0:T(8,128)(2,1)} async-done(((bf16[256,256]{1,0:T(8,128)(2,1)}), bf16[256,8192]{1,0:T(8,128)(2,1)}) %all-gather.4.cloned.1.call-update) | async-done | bytes 4194320 | tf_op jit(solution)/shard_map/all_gather | solution.py:30
  96.4 71.3 %all-gather.6.cloned.1.call-done = bf16[3,8192,256]{2,1,0:T(8,128)(2,1)} async-done(((bf16[3,1024,256]{2,1,0:T(8,128)(2,1)}), bf16[3,8192,256]{2,1,0:T(8,128)(2,1)}) %all-gather.6.cloned.1.call-update) | async-done | bytes 12582928 | tf_op jit(solution)/shard_map/all_gather | solution.py:34
  167.7 9.2 %fusion.2 = bf16[256,3,256]{2,0,1:T(8,128)(2,1)S(1)} fusion(bf16[3,8192,256]{2,1,0:T(8,128)(2,1)} %all-gather.6.cloned.1.call-done, bf16[256,8192]{1,0:T(8,128)(2,1)} %all-gather.4.cloned.1.call-done), kind=kOutput, calls=%fused_computation.2 | convolution fusion | flops 3221422080 | bytes 17170432 | tf_op jit(solution)/shard_map/td,idc->tic/dot_general | solution.py:31
  177.0 1.0 copy.41
  177.9 3.4 all-to-all-start
  181.4 0.2 fusion.52
  181.5 7.4 %all-to-all-done = f32[1,1,256,256]{3,1,0,2:T(1,128)S(1)} async-done(((f32[1,1,256,256]{3,1,0,2:T(1,128)}), f32[1,1,256,256]{3,1,0,2:T(1,128)S(1)}, u32[]{:S(2)}, u32[]{:S(2)}) %all-to-all-start) | async-done | bytes 262176 | tf_op jit(solution)/shard_map/all_to_all | solution.py:16
  188.9 0.7 convolution_negate_fusion
  189.6 0.8 add_bitcast_fusion.1
  190.5 0.1 pad_maximum_fusion
  190.5 1.6 copy.44
  192.1 3.6 %all-to-all-start.1 = ((f32[2,16,32,256]{3,2,0,1:T(8,128)}), f32[2,16,32,256]{3,2,0,1:T(8,128)S(1)}, u32[]{:S(2)}, u32[]{:S(2)}) async-start(f32[2,16,32,256]{3,2,0,1:T(8,128)} %copy.44), calls=%async_computation.1 | async-start | bytes 2097152 | tf_op jit(solution)/shard_map/all_to_all | solution.py:20
  195.7 0.2 all-gather.8.cloned.1.call-start
  195.9 1.3 fusion.124
  197.2 0.2 copy.64
  197.4 0.2 copy.65
  197.6 0.1 fusion.74
  197.8 13.8 %all-to-all-done.1 = f32[2,16,32,256]{3,2,0,1:T(8,128)S(1)} async-done(((f32[2,16,32,256]{3,2,0,1:T(8,128)}), f32[2,16,32,256]{3,2,0,1:T(8,128)S(1)}, u32[]{:S(2)}, u32[]{:S(2)}) %all-to-all-start.1) | async-done | bytes 1048608 | tf_op jit(solution)/shard_map/all_to_all | solution.py:20
  211.6 0.1 copy.45
  211.7 0.1 fusion.125
  211.9 1.8 fusion.24
  213.7 1.8 fusion.26
  215.6 1.8 fusion.5
  217.4 1.9 fusion.10
  219.3 1.6 fusion.16
  220.8 1.6 fusion.22
  222.4 1.8 convolution_add_fusion
  224.2 1.6 subtract_bitcast_fusion
  225.8 0.1 pad_maximum_fusion.1
  225.9 0.6 copy.54
  226.5 18.5 %all_to_all.48 = f32[2,2,256,256]{3,1,0,2:T(2,128)S(1)} all-to-all(f32[2,2,256,256]{3,1,0,2:T(2,128)S(1)} %copy.54), channel_id=1, replica_groups=mesh['ctx'=8,'tp'=32] {'ctx'}, dimensions={2} | all-to-all | bytes 2097152 | tf_op jit(solution)/shard_map/all_to_all | solution.py:16
  245.1 0.2 copy.55
  245.3 0.1 fusion.123
  245.4 0.4 copy.56
  245.8 0.4 squeeze.31
  246.2 0.4 fusion.58
  246.6 0.4 copy.57
  247.0 0.4 squeeze.32
  247.3 0.4 fusion.8
  247.8 0.1 copy.58
  247.9 9.9 %all_to_all.49 = f32[1,8,32,256]{3,2,0,1:T(8,128)S(1)} all-to-all(f32[1,8,32,256]{3,2,0,1:T(8,128)S(1)} %copy.58), channel_id=1, replica_groups=mesh['ctx'=8,'tp'=32] {'ctx'}, dimensions={1} | all-to-all | bytes 524288 | tf_op jit(solution)/shard_map/all_to_all | solution.py:20
  257.8 0.7 fusion.14
  258.5 0.0 all-gather.8.cloned.1.call-update
  258.6 83.5 %all-gather.8.cloned.1.call-done = bf16[256,8192]{1,0:T(8,128)(2,1)} async-done(((bf16[256,256]{1,0:T(8,128)(2,1)}), bf16[256,8192]{1,0:T(8,128)(2,1)}) %all-gather.8.cloned.1.call-update) | async-done | bytes 4194320 | tf_op jit(solution)/shard_map/all_gather | solution.py:111
  342.1 5.4 %convolution_convert_fusion = bf16[256,256]{1,0:T(8,128)(2,1)} fusion(bf16[256,8192]{1,0:T(8,128)(2,1)} %all-gather.8.cloned.1.call-done, bf16[8192,256]{1,0:T(8,128)(2,1)} %param.9), kind=kOutput, calls=%fused_computation.13 | convolution fusion | flops 1073807360 | bytes 8519680 | tf_op jit(solution)/shard_map/dot_general | solution.py:110
  (9 shorter events, 0.1 us)
Async XLA Ops:
  6.5 89.9 %all-gather.4.cloned.1.call-start = ((), (), s32[]{:S(2)}) async-start(), calls=%async_computation.4 | async-start | bytes 4325376 | tf_op jit(solution)/shard_map/all_gather | solution.py:30
  7.3 160.4 %all-gather.6.cloned.1.call-start = ((), (), s32[]{:S(2)}) async-start(), calls=%async_computation.5 | async-start | bytes 14155776 | tf_op jit(solution)/shard_map/all_gather | solution.py:34
  177.9 11.0 %all-to-all-start = ((f32[1,1,256,256]{3,1,0,2:T(1,128)}), f32[1,1,256,256]{3,1,0,2:T(1,128)S(1)}, u32[]{:S(2)}, u32[]{:S(2)}) async-start(f32[1,1,256,256]{3,1,0,2:T(1,128)} %copy.41), calls=%async_computation | async-start | bytes 524288 | tf_op jit(solution)/shard_map/all_to_all | solution.py:16
  192.1 19.4 %all-to-all-start.1 = ((f32[2,16,32,256]{3,2,0,1:T(8,128)}), f32[2,16,32,256]{3,2,0,1:T(8,128)S(1)}, u32[]{:S(2)}, u32[]{:S(2)}) async-start(f32[2,16,32,256]{3,2,0,1:T(8,128)} %copy.44), calls=%async_computation.1 | async-start | bytes 2097152 | tf_op jit(solution)/shard_map/all_to_all | solution.py:20
  195.7 146.3 %all-gather.8.cloned.1.call-start = ((), (), s32[]{:S(2)}) async-start(), calls=%async_computation.6 | async-start | bytes 4325376 | tf_op jit(solution)/shard_map/all_gather | solution.py:111
  245.3 12.5 %copy-start = (f32[256]{0:T(256)S(1)}, f32[256]{0:T(256)}, u32[]{:S(2)}) copy-start(f32[256]{0:T(256)} %param.8) | copy-start | bytes 3076
Sparse Core Ops, SparseCore 0:
  9.8 86.5 all-gather.3
  98.2 69.3 all-gather.5
  258.7 83.3 all-gather.7
where the time goes:
time: 355 us; the launch traced here: 354 us
  waiting for transfers between devices  266 us (75%)
  matrix products  30.8 us (9%)
  blocking collectives  28.5 us (8%)
  between operations  13.4 us (4%)
  starting transfers between devices  7.25 us (2%)
  local copies, waits for them, and re-layouts  7.09 us (2%)
    all_gather x1, waiting for transfers between devices, shards(): gathered = lax.all_gather(tokens, 'tp', axis=1, tiled=True)  88.4 us
    all_gather x1, waiting for transfers between devices, shards(): lax.all_gather(gated, 'tp', axis=1, tiled=True)  83.5 us
    all_gather x1, waiting for transfers between devices, shards(): lax.all_gather(in_weight, 'ctx', axis=1, tiled=True)  71.3 us
    all_to_all x1, blocking collectives, spread_step(): lax.all_to_all(values, 'ctx', split_axis=2, concat_axis=1, tiled=True)  18.5 us
    dot_general x12, matrix products, mult_high(): jnp.einsum(form, left, right, precision=lax.Precision.HIGHEST, preferred_...  16.2 us
    all_to_all x1, waiting for transfers between devices, collect_step(): lax.all_to_all(values, 'ctx', split_axis=1, concat_axis=2, tiled=True)  13.8 us
    all_to_all x1, blocking collectives, collect_step(): lax.all_to_all(values, 'ctx', split_axis=1, concat_axis=2, tiled=True)  9.95 us
    dot_general x1, matrix products, shards(): jnp.einsum('td,idc->tic', gathered, lax.all_gather(in_weight, 'ctx', axis...  9.25 us
  transfers between devices with their start and end apart: 5, of which 5 were waited for; matrix products, arithmetic and copies ran while one was open for 1% of the time, Pallas kernels for 0%

commit v1 on v0

v1 whole, which is shorter than its diff:
```python
import functools
import math

import jax
import jax.numpy as jnp
import numpy as np
from jax import lax
from jax.experimental import pallas as pl
from jax.experimental.pallas import tpu as pltpu
from jax.sharding import Mesh, PartitionSpec as P

NX, NC, NZ, NY = 4, 2, 8, 4
SIZES = dict(x=NX, core=NC, z=NZ, y=NY)
EVERY = ("x", "core", "z", "y")
CTX = ("x", "core")
HALF_CLASSES = 9


def place(x, core, z, y):
    return ((x * NC + core) * NZ + z) * NY + y


MOVE = [
    (place(p, core, 2 * x + f, y), place(x, core, 2 * p + f, y))
    for p in range(4)
    for core in range(2)
    for x in range(4)
    for f in range(2)
    for y in range(4)
]


def shift(values, axis, step):
    n = SIZES[axis]
    return lax.ppermute(values, axis, [(i, (i + step) % n) for i in range(n)])


def ring(values, axis):
    n = SIZES[axis]
    half = values.shape[0] // 2
    out = {0: values}
    up = down = values
    for k in range(1, n // 2):
        up, down = shift(up, axis, 1), shift(down, axis, -1)
        out[n - k], out[k] = up, down
    out[n // 2] = jnp.concatenate([shift(up[:half], axis, 1), shift(down[half:], axis, -1)], 0)
    return [out[k] for k in range(n)]


@functools.lru_cache(None)
def tables():
    r = np.arange(256)
    big = 2 * np.pi * (np.outer(r, r) % 256) / 256
    c, s = np.cos(big), np.sin(big)
    forward = np.block([[c, -s], [s, c]]).astype(np.float32)
    back = np.block([[c, s], [-s, c]]).astype(np.float32)
    j = np.arange(HALF_CLASSES)
    turn = 2 * np.pi * np.outer(j, r) / 4096
    twist = np.concatenate([np.cos(turn), np.sin(turn)], 1).astype(np.float32)
    return forward, back, twist[:, None, :]


def small(j, q):
    turn = 2 * math.pi * ((j * q) % 16) / 16
    return round(math.cos(turn), 12), round(math.sin(turn), 12)


def weighted(terms):
    total = None
    for scale, value in terms:
        if scale == 0.0:
            continue
        part = value if scale == 1.0 else -value if scale == -1.0 else scale * value
        total = part if total is None else total + part
    return total


def filter_kernel(
    place_ref, *refs,
):
    piece_refs = refs[:4]
    h_ref, skip_ref, forward_ref, back_ref, twist_ref, out_ref, drive, gate, left, right = refs[4:]
    spots = block_spots(place_ref[0])
    for spot, piece in zip(spots, piece_refs):
        for core in range(2):
            total = piece[core].astype(jnp.float32)
            for x in range(1, NX):
                total = total + piece[NC * x + core].astype(jnp.float32)
            q = 2 * spot + core
            gate[q] = total[0:32]
            drive[q] = total[32:64] * total[64:96]
    signal = [drive[q] for q in range(8)]
    for j in range(HALF_CLASSES):
        rows = slice(32 * j, 32 * j + 32)
        cos, sin = twist_ref[j, :, 0:256], twist_ref[j, :, 256:512]
        real = weighted([(small(j, q)[0], signal[q]) for q in range(8)])
        imag = weighted([(-small(j, q)[1], signal[q]) for q in range(8)])
        if imag is None:
            left[rows, 0:256] = real * cos
            left[rows, 256:512] = -real * sin
        else:
            left[rows, 0:256] = real * cos + imag * sin
            left[rows, 256:512] = imag * cos - real * sin
    right[...] = jnp.dot(
        left[...], forward_ref[...], precision=lax.Precision.HIGHEST,
        preferred_element_type=jnp.float32,
    )
    for j in range(HALF_CLASSES):
        rows = slice(32 * j, 32 * j + 32)
        h_real = h_ref[0, j].astype(jnp.float32)
        h_imag = h_ref[1, j].astype(jnp.float32)
        if 0 < j < 8:
            h_real = h_real + h_ref[0, 16 - j].astype(jnp.float32)
            h_imag = h_imag - h_ref[1, 16 - j].astype(jnp.float32)
        real, imag = right[rows, 0:256], right[rows, 256:512]
        left[rows, 0:256] = real * h_real - imag * h_imag
        left[rows, 256:512] = real * h_imag + imag * h_real
    right[...] = jnp.dot(
        left[...], back_ref[...], precision=lax.Precision.HIGHEST,
        preferred_element_type=jnp.float32,
    )
    reals, imags = [], []
    for j in range(HALF_CLASSES):
        rows = slice(32 * j, 32 * j + 32)
        cos, sin = twist_ref[j, :, 0:256], twist_ref[j, :, 256:512]
        real, imag = right[rows, 0:256], right[rows, 256:512]
        reals.append(real * cos - imag * sin)
        imags.append(real * sin + imag * cos)
    skip = skip_ref[...]
    for q in range(8):
        terms = [(small(j, q)[0], reals[j]) for j in range(HALF_CLASSES)]
        terms += [(-small(j, q)[1], imags[j]) for j in range(HALF_CLASSES)]
        convolved = weighted(terms) * (1.0 / 4096)
        out_ref[q] = (gate[q] * (convolved + skip * drive[q])).astype(out_ref.dtype)


def filtered(where, pieces, spectrum, skip):
    forward, back, twist = tables()
    vmem = pl.BlockSpec(memory_space=pltpu.VMEM)
    return pl.pallas_call(
        filter_kernel,
        out_shape=jax.ShapeDtypeStruct((8, 32, 256), jnp.bfloat16),
        in_specs=[pl.BlockSpec(memory_space=pltpu.SMEM)] + [vmem] * 9,
        out_specs=vmem,
        scratch_shapes=[
            pltpu.VMEM((8, 32, 256), jnp.float32),
            pltpu.VMEM((8, 32, 256), jnp.float32),
            pltpu.VMEM((32 * HALF_CLASSES, 512), jnp.float32),
            pltpu.VMEM((32 * HALF_CLASSES, 512), jnp.float32),
        ],
        compiler_params=pltpu.CompilerParams(vmem_limit_bytes=32 * 1024 * 1024),
    )(where, *pieces, spectrum, skip, forward, back, twist)


def spread_filter(filter_spectrum):
    first = 2 * (NC * lax.axis_index("x") + lax.axis_index("core"))
    eye = np.eye(256, dtype=np.float32)
    own = first + jnp.arange(2, dtype=jnp.int32)
    order = jnp.where((own <= 8)[:, None, None], eye[None], eye[None, :, ::-1])
    turned = jnp.einsum(
        "plgc,lgh->plch",
        filter_spectrum.astype(jnp.bfloat16),
        order.astype(jnp.bfloat16),
        preferred_element_type=jnp.float32,
    ).astype(jnp.bfloat16)
    turned = turned.reshape(2, 2, 8, 32, 256).transpose(2, 0, 1, 3, 4)
    spread = lax.all_to_all(turned, CTX, split_axis=0, concat_axis=0, tiled=True)
    return spread.transpose(1, 0, 2, 3, 4).reshape(2, 16, 32, 256)


def block_spots(z):
    own, side = z // 2, jnp.where(z % 2 == 0, -1, 1)
    return [own, (own + side) % 4, (own - side) % 4, (own + 2) % 4]


def turn_kernel(place_ref, weight_ref, out_ref):
    y = place_ref[1]
    for part in range(3):
        for k in range(4):
            block = weight_ref[part, (y + k) % 4].T
            for i in range(8):
                rows = slice(96 * i + 32 * part, 96 * i + 32 * part + 32)
                out_ref[rows, 256 * k : 256 * k + 256] = block[32 * i : 32 * i + 32]


def turned_weight(where, in_weight):
    vmem = pl.BlockSpec(memory_space=pltpu.VMEM)
    return pl.pallas_call(
        turn_kernel,
        out_shape=jax.ShapeDtypeStruct((768, 1024), jnp.bfloat16),
        in_specs=[pl.BlockSpec(memory_space=pltpu.SMEM), vmem],
        out_specs=vmem,
        compiler_params=pltpu.CompilerParams(vmem_limit_bytes=32 * 1024 * 1024),
    )(where, in_weight.reshape(3, 4, 256, 256))


def slot_kernel(steps, place_ref, *refs):
    units, (own_ref, other_ref, out_ref) = refs[:-3], refs[-3:]
    z, core = place_ref[0], place_ref[2]

    def project(unit, step):
        flip = (z + step + core) % 2
        weight = jnp.where(flip == 0, own_ref[...], other_ref[...])
        return lax.dot_general(
            weight, unit[...], (((1,), (1,)), ((), ())), preferred_element_type=jnp.float32
        )

    def put(first, second):
        total = project(first, steps[0]) + project(second, steps[1])
        out_ref[...] = total.astype(out_ref.dtype).reshape(8, 96, 256)

    if len(units) == 2:
        put(*units)
    else:
        lax.cond(z % 2 == 0, lambda: put(units[0], units[1]), lambda: put(units[2], units[3]))


def slot(where, steps, units, weights):
    vmem = pl.BlockSpec(memory_space=pltpu.VMEM)
    return pl.pallas_call(
        functools.partial(slot_kernel, steps),
        out_shape=jax.ShapeDtypeStruct((8, 96, 256), jnp.bfloat16),
        in_specs=[pl.BlockSpec(memory_space=pltpu.SMEM)] + [vmem] * (len(units) + 2),
        out_specs=vmem,
        compiler_params=pltpu.CompilerParams(vmem_limit_bytes=32 * 1024 * 1024),
    )(where, *units, *weights)


def mix_kernel(place_ref, *refs):
    blocks, weight_ref, out_ref = refs[:8], refs[8], refs[9]
    z, core = place_ref[0], place_ref[2]
    for column in range(4):
        total = jnp.zeros((256, 256), jnp.float32)
        for k in range(8):
            source = (z + k) % 8
            half = (source // 4 + core) % 2
            total += jnp.dot(
                blocks[k][...], weight_ref[half, column, source % 4],
                preferred_element_type=jnp.float32,
            )
        out_ref[column] = total.astype(out_ref.dtype)


def mix(where, blocks, weight):
    vmem = pl.BlockSpec(memory_space=pltpu.VMEM)
    return pl.pallas_call(
        mix_kernel,
        out_shape=jax.ShapeDtypeStruct((4, 256, 256), jnp.bfloat16),
        in_specs=[pl.BlockSpec(memory_space=pltpu.SMEM)] + [vmem] * 9,
        out_specs=vmem,
        compiler_params=pltpu.CompilerParams(vmem_limit_bytes=32 * 1024 * 1024),
    )(where, *blocks, weight)


def spread_weight(out_weight, core):
    halves = out_weight.reshape(2, 4, 4, 256, 256)
    own = lax.dynamic_index_in_dim(halves, core, 0, keepdims=False)
    own = lax.all_to_all(own.transpose(1, 0, 2, 3), "y", split_axis=0, concat_axis=0, tiled=True)
    return jnp.stack([own, shift(own, "core", 1)])


def shards(tokens, in_weight, filter_spectrum, skip_gain, out_weight):
    x, core = lax.axis_index("x"), lax.axis_index("core")
    z, y = lax.axis_index("z"), lax.axis_index("y")
    where = jnp.stack([z, y, core]).astype(jnp.int32)

    block = lax.ppermute(tokens, EVERY, MOVE)
    weight = turned_weight(where, in_weight)
    weights = weight, shift(weight, "core", 1)
    unit = jnp.concatenate(ring(block, "y"), 1)
    units = ring(unit, "z")
    spectrum = spread_filter(filter_spectrum)
    skip = lax.dynamic_slice_in_dim(skip_gain, 32 * (NC * x + core), 32)[:, None]
    out_weight = spread_weight(out_weight, core)
    slots = [
        ((0, 1), (units[0], units[1], units[0], units[7])),
        ((1, 2), (units[7], units[6], units[1], units[2])),
        ((2, 3), (units[2], units[3], units[6], units[5])),
        ((3, 4), (units[5], units[4], units[3], units[4])),
    ]
    pieces = [
        lax.all_to_all(
            slot(where, steps, used, weights), CTX, split_axis=0, concat_axis=0, tiled=True
        )
        for steps, used in slots
    ]
    gated = filtered(where, pieces, spectrum, skip)
    gated = lax.all_to_all(gated, CTX, split_axis=0, concat_axis=0, tiled=True)
    blocks = ring(gated.reshape(256, 256).T, "z")
    partial = mix(where, blocks, out_weight)
    parts = lax.all_to_all(partial, "y", split_axis=0, concat_axis=0, tiled=True)
    return jnp.sum(parts.astype(jnp.float32), 0).astype(jnp.bfloat16)


def solution(mesh):
    fine = Mesh(mesh.devices.reshape(NX, NC, NZ, NY), EVERY)
    tp = ("z", "y")
    placed = (P(CTX, tp), P(None, CTX, tp), P(None, CTX, None, tp), P(tp), P(None, tp))
    return jax.shard_map(
        shards, mesh=fine, in_specs=placed, out_specs=P(CTX, tp), check_vma=False
    )
```

time: 355 us -> 181 us (0.51)
  waiting for transfers between devices: 266 us -> 58.7 us
  starting transfers between devices: 7.25 us -> 61.5 us
  matrix products: 30.8 us -> 1.71 us
  Pallas kernels: 0 us -> 16.7 us
  between operations: 13.4 us -> 0.27 us
  blocking collectives: 28.5 us -> 18.8 us
  local copies, waits for them, and re-layouts: 7.09 us -> 15 us
  other arithmetic: 1.19 us -> 5.42 us
    all_gather x3 -> x0, waiting for transfers between devices: 243 us -> none  [the longest x1 88.4 us: shards(): gathered = lax.all_gather(tokens, 'tp', axis=1, tiled=True)]
    ppermute x0 -> x23, waiting for transfers between devices: none -> 46.7 us  [the longest x22 46.7 us: shift(): return lax.ppermute(values, axis, [(i, (i + step) % n) for i in range(n)])]
    ppermute x0 -> x23, starting transfers between devices: none -> 34.2 us  [the longest x22 33.5 us: shift(): return lax.ppermute(values, axis, [(i, (i + step) % n) for i in range(n)])]
    dot_general x14 -> x1, matrix products: 30.8 us -> 1.71 us  [spread_filter(): jnp.einsum('plgc,lgh->plch', filter_spectrum.astype(jnp.bfloat16), order....]
    all_to_all x2 -> x6, starting transfers between devices: 6.99 us -> 27.4 us  [the longest x4 16.6 us: shards(): lax.all_to_all(slot(where, steps, used, weights), CTX, split_axis=0, conc...]
    pallas_call x0 -> x7, Pallas kernels: none -> 16.7 us  [the longest x4 9.94 us: slot(): pl.pallas_call(functools.partial(slot_kernel, steps), out_shape=jax.Shape...]
    all_to_all x2, blocking collectives: 28.5 us -> 18.8 us  [the longest x1 10.3 us: shards(): lax.all_to_all(partial, 'y', split_axis=0, concat_axis=0, tiled=True)]
    all_to_all x2 -> x6, waiting for transfers between devices: 21.2 us -> 12 us  [the longest x4 12 us: shards(): lax.all_to_all(slot(where, steps, used, weights), CTX, split_axis=0, conc...]
  transfers between devices with their start and end apart: 5 -> 29, of which waited for: 5 -> 13; matrix products, arithmetic and copies ran while one was open for 1% -> 6% of each run, Pallas kernels for 0% -> 8%
where the time goes in v1:
time: 181 us; the launch traced here: 178 us
  starting transfers between devices  61.5 us (34%)
  waiting for transfers between devices  58.7 us (32%)
  blocking collectives  18.8 us (10%)
  Pallas kernels  16.7 us (9%)
  local copies, waits for them, and re-layouts  15 us (8%)
  other arithmetic  5.42 us (3%)
    ppermute x22, waiting for transfers between devices, shift(): return lax.ppermute(values, axis, [(i, (i + step) % n) for i in range(n)])  46.7 us
    ppermute x22, starting transfers between devices, shift(): return lax.ppermute(values, axis, [(i, (i + step) % n) for i in range(n)])  33.5 us
    all_to_all x4, starting transfers between devices, shards(): lax.all_to_all(slot(where, steps, used, weights), CTX, split_axis=0, conc...  16.6 us
    all_to_all x4, waiting for transfers between devices, shards(): lax.all_to_all(slot(where, steps, used, weights), CTX, split_axis=0, conc...  12 us
    all_to_all x1, blocking collectives, shards(): lax.all_to_all(partial, 'y', split_axis=0, concat_axis=0, tiled=True)  10.3 us
    pallas_call x4, Pallas kernels, slot(): pl.pallas_call(functools.partial(slot_kernel, steps), out_shape=jax.Shape...  9.94 us
    all_to_all x1, blocking collectives, shards(): gated = lax.all_to_all(gated, CTX, split_axis=0, concat_axis=0, tiled=True)  8.52 us
    all_to_all x1, starting transfers between devices, spread_weight(): lax.all_to_all(own.transpose(1, 0, 2, 3), 'y', split_axis=0, concat_axis=...  6.5 us
  transfers between devices with their start and end apart: 29, of which 13 were waited for; matrix products, arithmetic and copies ran while one was open for 6% of the time, Pallas kernels for 8%

profile of v1, /device:TPU:24, one launch (start us, length us, event | category | flops | bytes accessed | tf_op | source)
XLA Modules:
  0.0 178.2 jit_solution(5891982957715491398)
XLA Ops:
  0.0 3.1 %copy_bitcast_fusion = bf16[4,4,256,256]{3,2,1,0:T(8,128)(2,1)} fusion(bf16[2,4,4,256,256]{4,3,2,1,0:T(8,128)(2,1)} %bitcast.35, s32[]{:T(128)S(6)} %select_n.13), kind=kLoop, calls=%fused_computation.1 | loop fusion | bytes 4194308 | tf_op jit(solution)/shard_map/transpose | solution.py:258
  3.1 6.5 %all-to-all-start.6 = ((bf16[4,4,256,256]{3,2,1,0:T(8,128)(2,1)}), bf16[4,4,256,256]{3,2,1,0:T(8,128)(2,1)}, u32[]{:S(2)}, u32[]{:S(2)}) async-start(bf16[4,4,256,256]{3,2,1,0:T(8,128)(2,1)} %copy_bitcast_fusion), calls=%async_computation.6 | async-start | bytes 4194304 | tf_op jit(solution)/shard_map/all_to_all | solution.py:258
  9.7 1.0 shard_map.100.refs_4_
  11.7 2.0 %collective-permute-start.1 = (bf16[256,256]{1,0:T(8,128)(2,1)S(1)}, bf16[256,256]{1,0:T(8,128)(2,1)S(1)}, u32[]{:S(2)}, u32[]{:S(2)}) collective-permute-start(bf16[256,256]{1,0:T(8,128)(2,1)S(1)} %collective-permute-done), channel_id=1, source_target_pairs={{0,3},{1,0},{2,1},{3,2},{4,7},{5,4},{6,5},{7,6},{8,11},{9,8},{10,9... | collective-permute-start | bytes 393224 | tf_op jit(solution)/shard_map/ppermute | solution.py:35
  13.6 21.1 %collective-permute-done.2 = bf16[256,256]{1,0:T(8,128)(2,1)S(1)} collective-permute-done((bf16[256,256]{1,0:T(8,128)(2,1)S(1)}, bf16[256,256]{1,0:T(8,128)(2,1)S(1)}, u32[]{:S(2)}, u32[]{:S(2)}) %collective-permute-start.2) | collective-permute-done | bytes 131104 | tf_op jit(solution)/shard_map/ppermute | solution.py:35
  34.7 3.1 %collective-permute-start.3 = (bf16[128,256]{1,0:T(8,128)(2,1)S(1)}, bf16[128,256]{1,0:T(8,128)(2,1)S(1)}, u32[]{:S(2)}, u32[]{:S(2)}) collective-permute-start(bf16[128,256]{1,0:T(8,128)(2,1)S(1)} %slice.24), channel_id=1, source_target_pairs={{0,1},{1,2},{2,3},{3,0},{4,5},{5,6},{6,7},{7,4},{8,9},{9,10},{10,1... | collective-permute-start | bytes 196616 | tf_op jit(solution)/shard_map/ppermute | solution.py:35
  37.9 1.8 %collective-permute-done.3 = bf16[128,256]{1,0:T(8,128)(2,1)S(1)} collective-permute-done((bf16[128,256]{1,0:T(8,128)(2,1)S(1)}, bf16[128,256]{1,0:T(8,128)(2,1)S(1)}, u32[]{:S(2)}, u32[]{:S(2)}) %collective-permute-start.3) | collective-permute-done | bytes 65568 | tf_op jit(solution)/shard_map/ppermute | solution.py:35
  39.7 3.7 %collective-permute-done.4 = bf16[128,256]{1,0:T(8,128)(2,1)S(1)} collective-permute-done((bf16[128,256]{1,0:T(8,128)(2,1)S(1)}, bf16[128,256]{1,0:T(8,128)(2,1)S(1)}, u32[]{:S(2)}, u32[]{:S(2)}) %collective-permute-start.4) | collective-permute-done | bytes 65568 | tf_op jit(solution)/shard_map/ppermute | solution.py:35
  43.4 0.9 pad_maximum_fusion.1.refs_0_.refs_2_
  44.3 1.2 collective-permute-start.6
  45.5 4.2 %collective-permute-start.5 = (bf16[256,1024]{1,0:T(8,128)(2,1)}, bf16[256,1024]{1,0:T(8,128)(2,1)}, u32[]{:S(2)}, u32[]{:S(2)}) collective-permute-start(bf16[256,1024]{1,0:T(8,128)(2,1)} %pad_maximum_fusion.1.refs_0_.refs_2_), channel_id=1, source_target_pairs={{0,28},{4,0},{8,4},{12,8},{16,12},{20,16},{24,20},{28,24},{1,29},{... | collective-permute-start | bytes 1572872 | tf_op jit(solution)/shard_map/ppermute | solution.py:35
  49.6 1.7 convolution_convert_fusion
  51.4 0.8 copy.35
  52.2 4.3 %all-to-all-start.4 = ((bf16[8,2,2,32,256]{4,3,2,1,0:T(8,128)(2,1)}), bf16[8,2,2,32,256]{4,3,2,1,0:T(8,128)(2,1)}, u32[]{:S(2)}, u32[]{:S(2)}) async-start(bf16[8,2,2,32,256]{4,3,2,1,0:T(8,128)(2,1)} %bitcast.33), calls=%async_computation.4 | async-start | bytes 1048576 | tf_op jit(solution)/shard_map/all_to_all | solution.py:167
  56.5 4.1 %collective-permute-done.6.refs_3_.refs_0_ = bf16[256,1024]{1,0:T(8,128)(2,1)} collective-permute-done((bf16[256,1024]{1,0:T(8,128)(2,1)}, bf16[256,1024]{1,0:T(8,128)(2,1)}, u32[]{:S(2)}, u32[]{:S(2)}) %collective-permute-start.6) | collective-permute-done | bytes 524320 | tf_op jit(solution)/shard_map/ppermute | solution.py:35
  60.6 3.2 %collective-permute-start.9 = (bf16[256,1024]{1,0:T(8,128)(2,1)}, bf16[256,1024]{1,0:T(8,128)(2,1)}, u32[]{:S(2)}, u32[]{:S(2)}) collective-permute-start(bf16[256,1024]{1,0:T(8,128)(2,1)} %collective-permute-done.5.refs_1_.refs_2_), channel_id=1, source_target_pairs={{0,28},{4,0},{8,4},{12,8},{16,12},{20,16},{24,20},{28,24},{1,29},{... | collective-permute-start | bytes 1572872 | tf_op jit(solution)/shard_map/ppermute | solution.py:35
  63.9 2.6 %shard_map.101 = bf16[8,96,256]{2,1,0:T(8,128)(2,1)S(1)} custom-call(s32[3]{0:T(128)S(1)} %pad_add_fusion.place_ref, bf16[256,1024]{1,0:T(8,128)(2,1)} %pad_maximum_fusion.1.refs_0_.refs_2_, bf16[256,1024]{1,0:T(8,128)(2,1)} %collective-permute-done.5.refs_1_.refs_2_, bf16[256,1024]{1,0:T(8,128)(2,1)} %pad_maximum_fusion.1.refs_0_.refs_2_, ...), custom_call_target="tpu_custom_call" | custom-call | tf_op jit(solution)/shard_map/pallas_call | solution.py:220
  67.2 4.4 %all-to-all-start = ((bf16[8,96,256]{2,1,0:T(8,128)(2,1)}), bf16[8,96,256]{2,1,0:T(8,128)(2,1)S(1)}, u32[]{:S(2)}, u32[]{:S(2)}) async-start(bf16[8,96,256]{2,1,0:T(8,128)(2,1)} %copy-done.4), calls=%async_computation | async-start | bytes 786432 | tf_op jit(solution)/shard_map/all_to_all | solution.py:282
  71.6 2.3 %collective-permute-done.8.refs_1_.refs_2_ = bf16[256,1024]{1,0:T(8,128)(2,1)} collective-permute-done((bf16[256,1024]{1,0:T(8,128)(2,1)}, bf16[256,1024]{1,0:T(8,128)(2,1)}, u32[]{:S(2)}, u32[]{:S(2)}) %collective-permute-start.8) | collective-permute-done | bytes 524320 | tf_op jit(solution)/shard_map/ppermute | solution.py:35
  73.9 3.2 %collective-permute-start.10 = (bf16[256,1024]{1,0:T(8,128)(2,1)}, bf16[256,1024]{1,0:T(8,128)(2,1)}, u32[]{:S(2)}, u32[]{:S(2)}) collective-permute-start(bf16[256,1024]{1,0:T(8,128)(2,1)} %collective-permute-done.9.refs_3_.refs_0_), channel_id=1, source_target_pairs={{0,28},{4,0},{8,4},{12,8},{16,12},{20,16},{24,20},{28,24},{1,29},{... | collective-permute-start | bytes 1572872 | tf_op jit(solution)/shard_map/ppermute | solution.py:35
  77.2 2.6 %shard_map.102 = bf16[8,96,256]{2,1,0:T(8,128)(2,1)S(1)} custom-call(s32[3]{0:T(128)S(1)} %pad_add_fusion.place_ref, bf16[256,1024]{1,0:T(8,128)(2,1)} %collective-permute-done.6.refs_3_.refs_0_, bf16[256,1024]{1,0:T(8,128)(2,1)} %collective-permute-done.8.refs_1_.refs_2_, bf16[256,1024]{1,0:T(8,128)(2,1)} %collective-permute-done.5.refs_1_.refs_2_, ...), custom_call_target="tpu_custom_call" | custom-call | tf_op jit(solution)/shard_map/pallas_call | solution.py:220
  80.6 4.2 %all-to-all-start.1 = ((bf16[8,96,256]{2,1,0:T(8,128)(2,1)}), bf16[8,96,256]{2,1,0:T(8,128)(2,1)}, u32[]{:S(2)}, u32[]{:S(2)}) async-start(bf16[8,96,256]{2,1,0:T(8,128)(2,1)} %copy-done.2), calls=%async_computation.1 | async-start | bytes 786432 | tf_op jit(solution)/shard_map/all_to_all | solution.py:282
  84.8 2.7 %collective-permute-done.11.refs_3_.refs_0_ = bf16[256,1024]{1,0:T(8,128)(2,1)} collective-permute-done((bf16[256,1024]{1,0:T(8,128)(2,1)}, bf16[256,1024]{1,0:T(8,128)(2,1)}, u32[]{:S(2)}, u32[]{:S(2)}) %collective-permute-start.11) | collective-permute-done | bytes 524320 | tf_op jit(solution)/shard_map/ppermute | solution.py:35
  87.5 1.7 slice.26
  89.2 1.7 slice.27
  90.9 3.2 %collective-permute-start.13 = (bf16[128,1024]{1,0:T(8,128)(2,1)}, bf16[128,1024]{1,0:T(8,128)(2,1)}, u32[]{:S(2)}, u32[]{:S(2)}) collective-permute-start(bf16[128,1024]{1,0:T(8,128)(2,1)} %slice.27), channel_id=1, source_target_pairs={{0,28},{4,0},{8,4},{12,8},{16,12},{20,16},{24,20},{28,24},{1,29},{... | collective-permute-start | bytes 786440 | tf_op jit(solution)/shard_map/ppermute | solution.py:35
  94.1 2.6 %shard_map.103 = bf16[8,96,256]{2,1,0:T(8,128)(2,1)S(1)} custom-call(s32[3]{0:T(128)S(1)} %pad_add_fusion.place_ref, bf16[256,1024]{1,0:T(8,128)(2,1)} %collective-permute-done.9.refs_3_.refs_0_, bf16[256,1024]{1,0:T(8,128)(2,1)} %collective-permute-done.10.refs_1_.refs_2_, bf16[256,1024]{1,0:T(8,128)(2,1)} %collective-permute-done.8.refs_1_.refs_2_, ...), custom_call_target="tpu_custom_call" | custom-call | tf_op jit(solution)/shard_map/pallas_call | solution.py:220
  97.5 4.4 %all-to-all-start.2 = ((bf16[8,96,256]{2,1,0:T(8,128)(2,1)}), bf16[8,96,256]{2,1,0:T(8,128)(2,1)}, u32[]{:S(2)}, u32[]{:S(2)}) async-start(bf16[8,96,256]{2,1,0:T(8,128)(2,1)} %copy-done.3), calls=%async_computation.2 | async-start | bytes 786432 | tf_op jit(solution)/shard_map/all_to_all | solution.py:282
  101.9 1.1 pad_maximum_fusion.2.refs_1_.refs_3_
  103.0 2.3 %shard_map.104 = bf16[8,96,256]{2,1,0:T(8,128)(2,1)S(1)} custom-call(s32[3]{0:T(128)S(1)} %pad_add_fusion.place_ref, bf16[256,1024]{1,0:T(8,128)(2,1)} %collective-permute-done.11.refs_3_.refs_0_, bf16[256,1024]{1,0:T(8,128)(2,1)S(1)} %pad_maximum_fusion.2.refs_1_.refs_3_, bf16[256,1024]{1,0:T(8,128)(2,1)} %collective-permute-done.10.refs_1_.refs_2_, ...), custom_call_target="tpu_custom_call" | custom-call | tf_op jit(solution)/shard_map/pallas_call | solution.py:220
  106.0 4.9 %all-to-all-done.2.refs_2_ = bf16[8,96,256]{2,1,0:T(8,128)(2,1)} async-done(((bf16[8,96,256]{2,1,0:T(8,128)(2,1)}), bf16[8,96,256]{2,1,0:T(8,128)(2,1)}, u32[]{:S(2)}, u32[]{:S(2)}) %all-to-all-start.2) | async-done | bytes 393248 | tf_op jit(solution)/shard_map/all_to_all | solution.py:282
  111.0 3.5 %all-to-all-start.3 = ((bf16[8,96,256]{2,1,0:T(8,128)(2,1)}), bf16[8,96,256]{2,1,0:T(8,128)(2,1)S(1)}, u32[]{:S(2)}, u32[]{:S(2)}) async-start(bf16[8,96,256]{2,1,0:T(8,128)(2,1)} %copy-done.1), calls=%async_computation.3 | async-start | bytes 786432 | tf_op jit(solution)/shard_map/all_to_all | solution.py:282
  115.2 1.1 copy.23
  116.3 7.0 %all-to-all-done.3.refs_3_ = bf16[8,96,256]{2,1,0:T(8,128)(2,1)S(1)} async-done(((bf16[8,96,256]{2,1,0:T(8,128)(2,1)}), bf16[8,96,256]{2,1,0:T(8,128)(2,1)S(1)}, u32[]{:S(2)}, u32[]{:S(2)}) %all-to-all-start.3) | async-done | bytes 393248 | tf_op jit(solution)/shard_map/all_to_all | solution.py:282
  123.3 1.2 copy-done.7
  125.9 4.0 %shard_map.105 = bf16[8,32,256]{2,1,0:T(8,128)(2,1)S(1)} custom-call(s32[3]{0:T(128)S(1)} %pad_add_fusion.place_ref, bf16[8,96,256]{2,1,0:T(8,128)(2,1)S(1)} %all-to-all-done.refs_0_, bf16[8,96,256]{2,1,0:T(8,128)(2,1)} %all-to-all-done.1.refs_1_, bf16[8,96,256]{2,1,0:T(8,128)(2,1)} %all-to-all-done.2.refs_2_, ...), custom_call_target="tpu_custom_call" | custom-call | tf_op jit(solution)/shard_map/pallas_call | solution.py:140
  129.9 8.5 %all_to_all.40 = bf16[8,32,256]{2,1,0:T(8,128)(2,1)S(1)} all-to-all(bf16[8,32,256]{2,1,0:T(8,128)(2,1)S(1)} %shard_map.105), channel_id=1, replica_groups=mesh['x'=4,'core'=2,'z'=8,'y'=4] {'x','core'}, dimensions={0} | all-to-all | bytes 262144 | tf_op jit(solution)/shard_map/all_to_all | solution.py:288
  138.6 3.2 %collective-permute-start.14 = (bf16[256,256]{1,0:T(8,128)(2,1)S(1)}, bf16[256,256]{1,0:T(8,128)(2,1)S(1)}, u32[]{:S(2)}, u32[]{:S(2)}) collective-permute-start(bf16[256,256]{1,0:T(8,128)(2,1)S(1)} %bitcast.31), channel_id=1, source_target_pairs={{0,28},{4,0},{8,4},{12,8},{16,12},{20,16},{24,20},{28,24},{1,29},{... | collective-permute-start | bytes 393224 | tf_op jit(solution)/shard_map/ppermute | solution.py:35
  141.9 3.0 %collective-permute-done.17.refs_7_ = bf16[256,256]{1,0:T(8,128)(2,1)S(1)} collective-permute-done((bf16[256,256]{1,0:T(8,128)(2,1)S(1)}, bf16[256,256]{1,0:T(8,128)(2,1)S(1)}, u32[]{:S(2)}, u32[]{:S(2)}) %collective-permute-start.17) | collective-permute-done | bytes 131104 | tf_op jit(solution)/shard_map/ppermute | solution.py:35
  144.9 3.2 %collective-permute-start.15 = (bf16[256,256]{1,0:T(8,128)(2,1)S(1)}, bf16[256,256]{1,0:T(8,128)(2,1)S(1)}, u32[]{:S(2)}, u32[]{:S(2)}) collective-permute-start(bf16[256,256]{1,0:T(8,128)(2,1)S(1)} %collective-permute-done.14.refs_1_), channel_id=1, source_target_pairs={{0,28},{4,0},{8,4},{12,8},{16,12},{20,16},{24,20},{28,24},{1,29},{... | collective-permute-start | bytes 393224 | tf_op jit(solution)/shard_map/ppermute | solution.py:35
  148.1 2.9 %collective-permute-done.18.refs_6_ = bf16[256,256]{1,0:T(8,128)(2,1)S(1)} collective-permute-done((bf16[256,256]{1,0:T(8,128)(2,1)S(1)}, bf16[256,256]{1,0:T(8,128)(2,1)S(1)}, u32[]{:S(2)}, u32[]{:S(2)}) %collective-permute-start.18) | collective-permute-done | bytes 131104 | tf_op jit(solution)/shard_map/ppermute | solution.py:35
  151.1 3.2 %collective-permute-start.16 = (bf16[256,256]{1,0:T(8,128)(2,1)S(1)}, bf16[256,256]{1,0:T(8,128)(2,1)S(1)}, u32[]{:S(2)}, u32[]{:S(2)}) collective-permute-start(bf16[256,256]{1,0:T(8,128)(2,1)S(1)} %collective-permute-done.15.refs_2_), channel_id=1, source_target_pairs={{0,28},{4,0},{8,4},{12,8},{16,12},{20,16},{24,20},{28,24},{1,29},{... | collective-permute-start | bytes 393224 | tf_op jit(solution)/shard_map/ppermute | solution.py:35
  154.3 2.9 %collective-permute-done.19.refs_5_ = bf16[256,256]{1,0:T(8,128)(2,1)S(1)} collective-permute-done((bf16[256,256]{1,0:T(8,128)(2,1)S(1)}, bf16[256,256]{1,0:T(8,128)(2,1)S(1)}, u32[]{:S(2)}, u32[]{:S(2)}) %collective-permute-start.19) | collective-permute-done | bytes 131104 | tf_op jit(solution)/shard_map/ppermute | solution.py:35
  157.3 3.3 %collective-permute-start.21 = (bf16[128,256]{1,0:T(8,128)(2,1)S(1)}, bf16[128,256]{1,0:T(8,128)(2,1)S(1)}, u32[]{:S(2)}, u32[]{:S(2)}) collective-permute-start(bf16[128,256]{1,0:T(8,128)(2,1)S(1)} %slice.29), channel_id=1, source_target_pairs={{0,28},{4,0},{8,4},{12,8},{16,12},{20,16},{24,20},{28,24},{1,29},{... | collective-permute-start | bytes 196616 | tf_op jit(solution)/shard_map/ppermute | solution.py:35
  160.6 2.2 %collective-permute-done.20 = bf16[128,256]{1,0:T(8,128)(2,1)S(1)} collective-permute-done((bf16[128,256]{1,0:T(8,128)(2,1)S(1)}, bf16[128,256]{1,0:T(8,128)(2,1)S(1)}, u32[]{:S(2)}, u32[]{:S(2)}) %collective-permute-start.20) | collective-permute-done | bytes 65568 | tf_op jit(solution)/shard_map/ppermute | solution.py:35
  162.7 2.6 %pad_maximum_fusion.refs_8_ = bf16[2,4,4,256,256]{4,3,2,1,0:T(8,128)(2,1)S(1)} fusion(bf16[1,4,4,256,256]{4,3,2,1,0:T(8,128)(2,1)} %bitcast.18, bf16[1,4,4,256,256]{4,3,2,1,0:T(8,128)(2,1)} %bitcast.17), kind=kLoop, calls=%fused_computation | loop fusion | flops 2097152 | bytes 8388608 | tf_op jit(solution)/shard_map/stack | solution.py:259
  165.4 1.8 %shard_map.106 = bf16[4,256,256]{2,1,0:T(8,128)(2,1)S(1)} custom-call(s32[3]{0:T(128)S(1)} %pad_add_fusion.place_ref, bf16[256,256]{1,0:T(8,128)(2,1)S(1)} %bitcast.32, bf16[256,256]{1,0:T(8,128)(2,1)S(1)} %collective-permute-done.14.refs_1_, bf16[256,256]{1,0:T(8,128)(2,1)S(1)} %collective-permute-done.15.refs_2_, ...), custom_call_target="tpu_custom_call" | custom-call | tf_op jit(solution)/shard_map/pallas_call | solution.py:246
  167.2 10.3 %all_to_all.41 = bf16[4,256,256]{2,1,0:T(8,128)(2,1)S(1)} all-to-all(bf16[4,256,256]{2,1,0:T(8,128)(2,1)S(1)} %shard_map.106), channel_id=1, replica_groups=mesh['x'=4,'core'=2,'z'=8,'y'=4] {'y'}, dimensions={0} | all-to-all | bytes 1048576 | tf_op jit(solution)/shard_map/all_to_all | solution.py:291
  (63 shorter events, 7.4 us)
Async XLA Ops:
  0.0 114.4 %copy-start = (f32[256]{0:T(256)S(1)}, f32[256]{0:T(256)}, u32[]{:S(2)}) copy-start(f32[256]{0:T(256)} %param.13) | copy-start | bytes 3076
  3.1 6.6 %copy-start.5 = (bf16[3,1024,256]{2,1,0:T(8,128)(2,1)S(1)}, bf16[3,1024,256]{2,1,0:T(8,128)(2,1)}, u32[]{:S(2)}) copy-start(bf16[3,1024,256]{2,1,0:T(8,128)(2,1)} %param.11) | copy-start | bytes 4718596
  3.1 49.1 %all-to-all-start.6 = ((bf16[4,4,256,256]{3,2,1,0:T(8,128)(2,1)}), bf16[4,4,256,256]{3,2,1,0:T(8,128)(2,1)}, u32[]{:S(2)}, u32[]{:S(2)}) async-start(bf16[4,4,256,256]{3,2,1,0:T(8,128)(2,1)} %copy_bitcast_fusion), calls=%async_computation.6 | async-start | bytes 4194304 | tf_op jit(solution)/shard_map/all_to_all | solution.py:258
  9.6 1.2 copy-start.11
  9.7 40.0 %copy-start.10 = (bf16[256,256]{1,0:T(8,128)(2,1)S(1)}, bf16[256,256]{1,0:T(8,128)(2,1)}, u32[]{:S(2)}) copy-start(bf16[256,256]{1,0:T(8,128)(2,1)} %constant.68) | copy-start | bytes 393220
  10.7 53.1 %collective-permute-start.7 = (bf16[768,1024]{1,0:T(8,128)(2,1)S(1)}, bf16[768,1024]{1,0:T(8,128)(2,1)S(1)}, u32[]{:S(2)}, u32[]{:S(2)}) collective-permute-start(bf16[768,1024]{1,0:T(8,128)(2,1)S(1)} %shard_map.100.refs_4_), channel_id=1, source_target_pairs={{0,32},{32,0},{1,33},{33,1},{2,34},{34,2},{3,35},{35,3},{4,36},{36... | collective-permute-start | bytes 4718600 | tf_op jit(solution)/shard_map/ppermute | solution.py:35
  10.8 0.7 collective-permute-start
  11.5 23.2 %collective-permute-start.2 = (bf16[256,256]{1,0:T(8,128)(2,1)S(1)}, bf16[256,256]{1,0:T(8,128)(2,1)S(1)}, u32[]{:S(2)}, u32[]{:S(2)}) collective-permute-start(bf16[256,256]{1,0:T(8,128)(2,1)S(1)} %collective-permute-done), channel_id=1, source_target_pairs={{0,1},{1,2},{2,3},{3,0},{4,5},{5,6},{6,7},{7,4},{8,9},{9,10},{10,1... | collective-permute-start | bytes 393224 | tf_op jit(solution)/shard_map/ppermute | solution.py:35
  11.7 26.1 %collective-permute-start.1 = (bf16[256,256]{1,0:T(8,128)(2,1)S(1)}, bf16[256,256]{1,0:T(8,128)(2,1)S(1)}, u32[]{:S(2)}, u32[]{:S(2)}) collective-permute-start(bf16[256,256]{1,0:T(8,128)(2,1)S(1)} %collective-permute-done), channel_id=1, source_target_pairs={{0,3},{1,0},{2,1},{3,2},{4,7},{5,4},{6,5},{7,6},{8,11},{9,8},{10,9... | collective-permute-start | bytes 393224 | tf_op jit(solution)/shard_map/ppermute | solution.py:35
  34.7 5.0 %collective-permute-start.3 = (bf16[128,256]{1,0:T(8,128)(2,1)S(1)}, bf16[128,256]{1,0:T(8,128)(2,1)S(1)}, u32[]{:S(2)}, u32[]{:S(2)}) collective-permute-start(bf16[128,256]{1,0:T(8,128)(2,1)S(1)} %slice.24), channel_id=1, source_target_pairs={{0,1},{1,2},{2,3},{3,0},{4,5},{5,6},{6,7},{7,4},{8,9},{9,10},{10,1... | collective-permute-start | bytes 196616 | tf_op jit(solution)/shard_map/ppermute | solution.py:35
  37.8 5.6 %collective-permute-start.4 = (bf16[128,256]{1,0:T(8,128)(2,1)S(1)}, bf16[128,256]{1,0:T(8,128)(2,1)S(1)}, u32[]{:S(2)}, u32[]{:S(2)}) collective-permute-start(bf16[128,256]{1,0:T(8,128)(2,1)S(1)} %slice.25), channel_id=1, source_target_pairs={{0,3},{1,0},{2,1},{3,2},{4,7},{5,4},{6,5},{7,6},{8,11},{9,8},{10,9... | collective-permute-start | bytes 196616 | tf_op jit(solution)/shard_map/ppermute | solution.py:35
  44.3 16.4 %collective-permute-start.6 = (bf16[256,1024]{1,0:T(8,128)(2,1)}, bf16[256,1024]{1,0:T(8,128)(2,1)}, u32[]{:S(2)}, u32[]{:S(2)}) collective-permute-start(bf16[256,1024]{1,0:T(8,128)(2,1)} %pad_maximum_fusion.1.refs_0_.refs_2_), channel_id=1, source_target_pairs={{0,4},{4,8},{8,12},{12,16},{16,20},{20,24},{24,28},{28,0},{1,5},{5... | collective-permute-start | bytes 1572872 | tf_op jit(solution)/shard_map/ppermute | solution.py:35
  45.5 15.1 %collective-permute-start.5 = (bf16[256,1024]{1,0:T(8,128)(2,1)}, bf16[256,1024]{1,0:T(8,128)(2,1)}, u32[]{:S(2)}, u32[]{:S(2)}) collective-permute-start(bf16[256,1024]{1,0:T(8,128)(2,1)} %pad_maximum_fusion.1.refs_0_.refs_2_), channel_id=1, source_target_pairs={{0,28},{4,0},{8,4},{12,8},{16,12},{20,16},{24,20},{28,24},{1,29},{... | collective-permute-start | bytes 1572872 | tf_op jit(solution)/shard_map/ppermute | solution.py:35
  52.2 15.0 %all-to-all-start.4 = ((bf16[8,2,2,32,256]{4,3,2,1,0:T(8,128)(2,1)}), bf16[8,2,2,32,256]{4,3,2,1,0:T(8,128)(2,1)}, u32[]{:S(2)}, u32[]{:S(2)}) async-start(bf16[8,2,2,32,256]{4,3,2,1,0:T(8,128)(2,1)} %bitcast.33), calls=%async_computation.4 | async-start | bytes 1048576 | tf_op jit(solution)/shard_map/all_to_all | solution.py:167
  60.6 13.3 %collective-permute-start.8 = (bf16[256,1024]{1,0:T(8,128)(2,1)}, bf16[256,1024]{1,0:T(8,128)(2,1)}, u32[]{:S(2)}, u32[]{:S(2)}) collective-permute-start(bf16[256,1024]{1,0:T(8,128)(2,1)} %collective-permute-done.6.refs_3_.refs_0_), channel_id=1, source_target_pairs={{0,4},{4,8},{8,12},{12,16},{16,20},{20,24},{24,28},{28,0},{1,5},{5... | collective-permute-start | bytes 1572872 | tf_op jit(solution)/shard_map/ppermute | solution.py:35
  60.6 13.3 %collective-permute-start.9 = (bf16[256,1024]{1,0:T(8,128)(2,1)}, bf16[256,1024]{1,0:T(8,128)(2,1)}, u32[]{:S(2)}, u32[]{:S(2)}) collective-permute-start(bf16[256,1024]{1,0:T(8,128)(2,1)} %collective-permute-done.5.refs_1_.refs_2_), channel_id=1, source_target_pairs={{0,28},{4,0},{8,4},{12,8},{16,12},{20,16},{24,20},{28,24},{1,29},{... | collective-permute-start | bytes 1572872 | tf_op jit(solution)/shard_map/ppermute | solution.py:35
  63.9 98.9 %collective-permute-start.22 = (bf16[4,4,256,256]{3,2,1,0:T(8,128)(2,1)}, bf16[4,4,256,256]{3,2,1,0:T(8,128)(2,1)}, u32[]{:S(2)}, u32[]{:S(2)}) collective-permute-start(bf16[4,4,256,256]{3,2,1,0:T(8,128)(2,1)} %all-to-all-done.6), channel_id=1, source_target_pairs={{0,32},{32,0},{1,33},{33,1},{2,34},{34,2},{3,35},{35,3},{4,36},{36... | collective-permute-start | bytes 6291464 | tf_op jit(solution)/shard_map/ppermute | solution.py:35
  66.4 0.8 copy-start.4
  67.2 13.4 %all-to-all-start = ((bf16[8,96,256]{2,1,0:T(8,128)(2,1)}), bf16[8,96,256]{2,1,0:T(8,128)(2,1)S(1)}, u32[]{:S(2)}, u32[]{:S(2)}) async-start(bf16[8,96,256]{2,1,0:T(8,128)(2,1)} %copy-done.4), calls=%async_computation | async-start | bytes 786432 | tf_op jit(solution)/shard_map/all_to_all | solution.py:282
  73.9 13.6 %collective-permute-start.11 = (bf16[256,1024]{1,0:T(8,128)(2,1)}, bf16[256,1024]{1,0:T(8,128)(2,1)}, u32[]{:S(2)}, u32[]{:S(2)}) collective-permute-start(bf16[256,1024]{1,0:T(8,128)(2,1)} %collective-permute-done.8.refs_1_.refs_2_), channel_id=1, source_target_pairs={{0,4},{4,8},{8,12},{12,16},{16,20},{20,24},{24,28},{28,0},{1,5},{5... | collective-permute-start | bytes 1572872 | tf_op jit(solution)/shard_map/ppermute | solution.py:35
  73.9 15.3 %collective-permute-start.10 = (bf16[256,1024]{1,0:T(8,128)(2,1)}, bf16[256,1024]{1,0:T(8,128)(2,1)}, u32[]{:S(2)}, u32[]{:S(2)}) collective-permute-start(bf16[256,1024]{1,0:T(8,128)(2,1)} %collective-permute-done.9.refs_3_.refs_0_), channel_id=1, source_target_pairs={{0,28},{4,0},{8,4},{12,8},{16,12},{20,16},{24,20},{28,24},{1,29},{... | collective-permute-start | bytes 1572872 | tf_op jit(solution)/shard_map/ppermute | solution.py:35
  79.7 0.8 copy-start.2
  80.6 16.9 %all-to-all-start.1 = ((bf16[8,96,256]{2,1,0:T(8,128)(2,1)}), bf16[8,96,256]{2,1,0:T(8,128)(2,1)}, u32[]{:S(2)}, u32[]{:S(2)}) async-start(bf16[8,96,256]{2,1,0:T(8,128)(2,1)} %copy-done.2), calls=%async_computation.1 | async-start | bytes 786432 | tf_op jit(solution)/shard_map/all_to_all | solution.py:282
  89.2 12.7 %collective-permute-start.12 = (bf16[128,1024]{1,0:T(8,128)(2,1)}, bf16[128,1024]{1,0:T(8,128)(2,1)}, u32[]{:S(2)}, u32[]{:S(2)}) collective-permute-start(bf16[128,1024]{1,0:T(8,128)(2,1)} %slice.26), channel_id=1, source_target_pairs={{0,4},{4,8},{8,12},{12,16},{16,20},{20,24},{24,28},{28,0},{1,5},{5... | collective-permute-start | bytes 786440 | tf_op jit(solution)/shard_map/ppermute | solution.py:35
  90.9 11.0 %collective-permute-start.13 = (bf16[128,1024]{1,0:T(8,128)(2,1)}, bf16[128,1024]{1,0:T(8,128)(2,1)}, u32[]{:S(2)}, u32[]{:S(2)}) collective-permute-start(bf16[128,1024]{1,0:T(8,128)(2,1)} %slice.27), channel_id=1, source_target_pairs={{0,28},{4,0},{8,4},{12,8},{16,12},{20,16},{24,20},{28,24},{1,29},{... | collective-permute-start | bytes 786440 | tf_op jit(solution)/shard_map/ppermute | solution.py:35
  96.7 0.8 copy-start.3
  97.5 13.5 %all-to-all-start.2 = ((bf16[8,96,256]{2,1,0:T(8,128)(2,1)}), bf16[8,96,256]{2,1,0:T(8,128)(2,1)}, u32[]{:S(2)}, u32[]{:S(2)}) async-start(bf16[8,96,256]{2,1,0:T(8,128)(2,1)} %copy-done.3), calls=%async_computation.2 | async-start | bytes 786432 | tf_op jit(solution)/shard_map/all_to_all | solution.py:282
  105.3 0.8 copy-start.1
  106.0 17.2 %copy-start.6 = (f32[512,512]{1,0:T(8,128)S(1)}, f32[512,512]{1,0:T(8,128)}, u32[]{:S(2)}) copy-start(f32[512,512]{1,0:T(8,128)} %constant.49.clone.refs_7_) | copy-start | bytes 3145732
  111.0 12.3 %all-to-all-start.3 = ((bf16[8,96,256]{2,1,0:T(8,128)(2,1)}), bf16[8,96,256]{2,1,0:T(8,128)(2,1)S(1)}, u32[]{:S(2)}, u32[]{:S(2)}) async-start(bf16[8,96,256]{2,1,0:T(8,128)(2,1)} %copy-done.1), calls=%async_computation.3 | async-start | bytes 786432 | tf_op jit(solution)/shard_map/all_to_all | solution.py:282
  123.3 1.2 copy-start.7
  124.5 0.7 copy-start.8
  125.2 0.7 copy-start.9
  138.5 6.3 %collective-permute-start.17 = (bf16[256,256]{1,0:T(8,128)(2,1)S(1)}, bf16[256,256]{1,0:T(8,128)(2,1)S(1)}, u32[]{:S(2)}, u32[]{:S(2)}) collective-permute-start(bf16[256,256]{1,0:T(8,128)(2,1)S(1)} %bitcast.30), channel_id=1, source_target_pairs={{0,4},{4,8},{8,12},{12,16},{16,20},{20,24},{24,28},{28,0},{1,5},{5... | collective-permute-start | bytes 393224 | tf_op jit(solution)/shard_map/ppermute | solution.py:35
  138.6 6.3 %collective-permute-start.14 = (bf16[256,256]{1,0:T(8,128)(2,1)S(1)}, bf16[256,256]{1,0:T(8,128)(2,1)S(1)}, u32[]{:S(2)}, u32[]{:S(2)}) collective-permute-start(bf16[256,256]{1,0:T(8,128)(2,1)S(1)} %bitcast.31), channel_id=1, source_target_pairs={{0,28},{4,0},{8,4},{12,8},{16,12},{20,16},{24,20},{28,24},{1,29},{... | collective-permute-start | bytes 393224 | tf_op jit(solution)/shard_map/ppermute | solution.py:35
  144.9 6.2 %collective-permute-start.18 = (bf16[256,256]{1,0:T(8,128)(2,1)S(1)}, bf16[256,256]{1,0:T(8,128)(2,1)S(1)}, u32[]{:S(2)}, u32[]{:S(2)}) collective-permute-start(bf16[256,256]{1,0:T(8,128)(2,1)S(1)} %collective-permute-done.17.refs_7_), channel_id=1, source_target_pairs={{0,4},{4,8},{8,12},{12,16},{16,20},{20,24},{24,28},{28,0},{1,5},{5... | collective-permute-start | bytes 393224 | tf_op jit(solution)/shard_map/ppermute | solution.py:35
  144.9 6.2 %collective-permute-start.15 = (bf16[256,256]{1,0:T(8,128)(2,1)S(1)}, bf16[256,256]{1,0:T(8,128)(2,1)S(1)}, u32[]{:S(2)}, u32[]{:S(2)}) collective-permute-start(bf16[256,256]{1,0:T(8,128)(2,1)S(1)} %collective-permute-done.14.refs_1_), channel_id=1, source_target_pairs={{0,28},{4,0},{8,4},{12,8},{16,12},{20,16},{24,20},{28,24},{1,29},{... | collective-permute-start | bytes 393224 | tf_op jit(solution)/shard_map/ppermute | solution.py:35
  151.1 6.2 %collective-permute-start.19 = (bf16[256,256]{1,0:T(8,128)(2,1)S(1)}, bf16[256,256]{1,0:T(8,128)(2,1)S(1)}, u32[]{:S(2)}, u32[]{:S(2)}) collective-permute-start(bf16[256,256]{1,0:T(8,128)(2,1)S(1)} %collective-permute-done.18.refs_6_), channel_id=1, source_target_pairs={{0,4},{4,8},{8,12},{12,16},{16,20},{20,24},{24,28},{28,0},{1,5},{5... | collective-permute-start | bytes 393224 | tf_op jit(solution)/shard_map/ppermute | solution.py:35
  151.1 6.2 %collective-permute-start.16 = (bf16[256,256]{1,0:T(8,128)(2,1)S(1)}, bf16[256,256]{1,0:T(8,128)(2,1)S(1)}, u32[]{:S(2)}, u32[]{:S(2)}) collective-permute-start(bf16[256,256]{1,0:T(8,128)(2,1)S(1)} %collective-permute-done.15.refs_2_), channel_id=1, source_target_pairs={{0,28},{4,0},{8,4},{12,8},{16,12},{20,16},{24,20},{28,24},{1,29},{... | collective-permute-start | bytes 393224 | tf_op jit(solution)/shard_map/ppermute | solution.py:35
  157.2 5.5 %collective-permute-start.20 = (bf16[128,256]{1,0:T(8,128)(2,1)S(1)}, bf16[128,256]{1,0:T(8,128)(2,1)S(1)}, u32[]{:S(2)}, u32[]{:S(2)}) collective-permute-start(bf16[128,256]{1,0:T(8,128)(2,1)S(1)} %slice.28), channel_id=1, source_target_pairs={{0,4},{4,8},{8,12},{12,16},{16,20},{20,24},{24,28},{28,0},{1,5},{5... | collective-permute-start | bytes 196616 | tf_op jit(solution)/shard_map/ppermute | solution.py:35
  157.3 5.4 %collective-permute-start.21 = (bf16[128,256]{1,0:T(8,128)(2,1)S(1)}, bf16[128,256]{1,0:T(8,128)(2,1)S(1)}, u32[]{:S(2)}, u32[]{:S(2)}) collective-permute-start(bf16[128,256]{1,0:T(8,128)(2,1)S(1)} %slice.29), channel_id=1, source_target_pairs={{0,28},{4,0},{8,4},{12,8},{16,12},{20,16},{24,20},{28,24},{1,29},{... | collective-permute-start | bytes 196616 | tf_op jit(solution)/shard_map/ppermute | solution.py:35
